TPU v7x, 512 devices: a whole 4x4x16 slice. The times are simulated.
512 devices in a mesh: test: 8 (over z_lo, core), slab: 64 (over y, x, z_hi).
Axes of the slice: x: 4, y: 4, z: 16 (z_hi: 4, z_lo: 4; z = z_hi * 4 + z_lo), core: 2. Of those that a mesh axis runs over, the one named last changes fastest.
Arguments:
- log_conductivity: float32 [128, 512, 128], P('slab'), may hold values from -4 to 4
- storage: float32 [128, 512, 128], P('slab'), may hold values from 0.1 to 1
- active_mask: int32 [128, 512, 128], P('slab'), may hold values 0 or 1
- heads: float32 [8, 128, 512, 128], P('test', 'slab'), may hold values from -6 to 6
- adjoint_next: float32 [8, 128, 512, 128], P('test', 'slab'), may hold values from -6 to 6
- pump_cells: int32 [8], P('test'), may hold values from 0 to 8388607
- obs_cells: int32 [64], replicated, may hold values from 0 to 8388607
- obs_data: float32 [8, 64], P('test'), may hold values from -6 to 6
Outputs:
- adjoint: float32 [8, 128, 512, 128], P('test', 'slab')
- gradient: float32 [128, 512, 128], P('slab')
All inputs are finite; a program needn't handle non-finite values. No bound on the sum of `active_mask` on one device may be relied on, other than what follows from the above.
Results may differ from a plain program's by a relative error of at most 0.0003.
Values sent between devices are 32-bit elements; how exact they have to be, the bound alone decides.
A program may use at most 64 MiB of HBM per device.

v0:
```python
import jax
import jax.numpy as jnp
from jax import lax
from jax.sharding import PartitionSpec as P

ITERS = 3


WELL_TERM = 4.0


def padded_2(cells, sides, width):
    for axis, dim in sides:
        count = lax.axis_size(axis)
        ends = count - 1
        head = lax.slice_in_dim(cells, 0, width, axis=dim)
        tail = lax.slice_in_dim(cells, cells.shape[dim] - width, cells.shape[dim], axis=dim)
        cells = jnp.concatenate(
            [
                lax.ppermute(tail, axis, [(i, (i + 1) % count) for i in range(ends)]),
                cells,
                lax.ppermute(head, axis, [((i + 1) % count, i) for i in range(ends)]),
            ],
            axis=dim,
        )
    return cells


def part_of(v, axis_num, start, length):
    return lax.slice_in_dim(v, start, start + length, axis=axis_num)


def pad_axis(v, axis_num):
    widths = [(0, 0)] * v.ndim
    widths[axis_num] = (1, 1)
    return jnp.pad(v, widths)


def face_values(cond_pad, axis_num):
    count = cond_pad.shape[axis_num] - 1
    left = part_of(cond_pad, axis_num, 0, count)
    right = part_of(cond_pad, axis_num, 1, count)
    return 2.0 * left * right / (left + right)


def flux_axis(padded, faces, axis_num):
    count = padded.shape[axis_num] - 1
    terms = faces * (part_of(padded, axis_num, 0, count) - part_of(padded, axis_num, 1, count))
    return part_of(terms, axis_num, 1, count - 1) - part_of(terms, axis_num, 0, count - 1)


def face_total(faces, axis_num):
    count = faces.shape[axis_num] - 1
    return part_of(faces, axis_num, 1, count) + part_of(faces, axis_num, 0, count)


def slope(own, other):
    total = own + other
    return 2.0 * own * other * other / (total * total)


def side_terms(cond_pad, adj_pad, head_pad, axis_num):
    count = cond_pad.shape[axis_num] - 2
    cond_c = part_of(cond_pad, axis_num, 1, count)
    adj_c = part_of(adj_pad, axis_num, 1, count)
    head_c = part_of(head_pad, axis_num, 1, count)
    total = jnp.zeros(cond_c.shape, jnp.float32)
    for start in (0, 2):
        cond_n = part_of(cond_pad, axis_num, start, count)
        adj_n = part_of(adj_pad, axis_num, start, count)
        head_n = part_of(head_pad, axis_num, start, count)
        total = total + slope(cond_c, cond_n) * (adj_c - adj_n) * (head_c - head_n)
    return total


def operate(field, faces, self_term, active):
    field_x = padded_2(field, (("slab", 0),), 1)
    flux = flux_axis(field_x, faces[0], 0)
    flux = flux + flux_axis(pad_axis(field, 1), faces[1], 1)
    flux = flux + flux_axis(pad_axis(field, 2), faces[2], 2)
    return (active * (self_term * field + flux) + (1.0 - active) * field, field_x)


def precond_inner(resid, precond):
    return lax.psum(jnp.sum(resid * precond), "slab")


def on_device(
    log_conductivity, storage, active_mask, heads, adjoint_next, pump_cells, obs_cells, obs_data
):
    width, rows, depth = log_conductivity.shape
    conduct = jnp.exp(log_conductivity)
    active = active_mask.astype(jnp.float32)
    heads_here = heads[0]
    later = adjoint_next[0]
    stacked = padded_2(jnp.stack([conduct, heads_here]), (("slab", 1),), 1)
    cond_x = stacked[0]
    heads_x = stacked[1]
    cond_y = pad_axis(conduct, 1)
    cond_z = pad_axis(conduct, 2)
    faces = (face_values(cond_x, 0), face_values(cond_y, 1), face_values(cond_z, 2))
    face_sum = face_total(faces[0], 0) + face_total(faces[1], 1) + face_total(faces[2], 2)
    shape = (width, rows, depth)
    cells_here = width * rows * depth
    offset = lax.axis_index("slab") * cells_here
    local_index = (
        lax.broadcasted_iota(jnp.int32, shape, 0) * (rows * depth)
        + lax.broadcasted_iota(jnp.int32, shape, 1) * depth
        + lax.broadcasted_iota(jnp.int32, shape, 2)
    )
    well = jnp.where(local_index == pump_cells[0] - offset, WELL_TERM, 0.0).astype(jnp.float32)
    self_term = storage + well
    diag = active * (self_term + face_sum) + (1.0 - active)
    obs_local = obs_cells - offset
    inside = (obs_local >= 0) & (obs_local < cells_here)
    safe_index = jnp.where(inside, obs_local, 0)
    picked = heads_here.reshape(-1)[safe_index]
    values = jnp.where(inside, picked - obs_data[0], 0.0)
    misfit = jnp.zeros((cells_here,), jnp.float32).at[safe_index].add(values).reshape(shape)
    rhs = active * (storage * later + misfit)
    solution = jnp.zeros_like(rhs)
    resid = rhs
    low_rim = jnp.zeros((rows, depth), jnp.float32)
    high_rim = jnp.zeros((rows, depth), jnp.float32)
    precond = resid / diag
    direction = precond
    rz_now = precond_inner(resid, precond)
    for step in range(ITERS):
        image, dir_x = operate(direction, faces, self_term, active)
        alpha = rz_now / lax.psum(jnp.sum(direction * image), "slab")
        solution = solution + alpha * direction
        low_rim = low_rim + alpha * dir_x[0]
        high_rim = high_rim + alpha * dir_x[-1]
        resid = resid - alpha * image
        if step + 1 < ITERS:
            precond = resid / diag
            rz_next = precond_inner(resid, precond)
            direction = precond + rz_next / rz_now * direction
            rz_now = rz_next
    solution_x = padded_2(solution, (("slab", 0),), 1)
    terms = side_terms(cond_x, solution_x, heads_x, 0)
    terms = terms + side_terms(cond_y, pad_axis(solution, 1), pad_axis(heads_here, 1), 1)
    terms = terms + side_terms(cond_z, pad_axis(solution, 2), pad_axis(heads_here, 2), 2)
    gradient = lax.psum(-terms, "test")
    return (solution[None], gradient)


def solution(mesh):
    return jax.shard_map(
        on_device,
        mesh=mesh,
        in_specs=(
            P("slab", None, None),
            P("slab", None, None),
            P("slab", None, None),
            P("test", "slab", None, None),
            P("test", "slab", None, None),
            P("test"),
            P(),
            P("test", None),
        ),
        out_specs=(P("test", "slab", None, None), P("slab", None, None)),
        check_vma=False,
    )
```

profile of v0, /device:TPU:1, one launch (start us, length us, event | category | flops | bytes accessed | tf_op | source)
XLA Modules:
  0.0 1364.3 jit_solution(6113851860813788381)
XLA Ops:
  7.2 0.0 all-reduce.15.cloned.1.call-start
  7.2 1.2 exponential_bitcast_fusion
  8.4 0.0 copy-start.16
  8.4 0.9 fusion.32
  9.3 9.7 collective-permute-start
  19.0 1.3 collective-permute-start.1
  20.3 0.8 gather_fusion
  21.7 1.8 scatter_custom_fusion
  23.5 0.1 add_divide_fusion.2
  23.7 0.3 add_divide_fusion
  24.0 12.1 collective-permute-done
  36.1 37.3 %collective-permute-done.1 = f32[2,1,512,128]{3,2,1,0:T(8,128)S(1)} collective-permute-done((f32[2,1,512,128]{3,2,1,0:T(8,128)S(1)}, f32[2,1,512,128]{3,2,1,0:T(8,128)S(1)}, u32[]{:S(2)}, u32[]{:S(2)}) %collective-permute-start.1) | collective-permute-done | bytes 524320 | tf_op jit(solution)/shard_map/ppermute | solution.py:22
  73.4 0.2 maximum_maximum_fusion
  73.6 0.0 copy-start.2
  73.6 0.0 copy-start.14
  73.7 0.1 add_divide_fusion.1
  73.8 0.9 copy-done.8
  74.8 0.3 copy-done.2
  75.1 0.6 copy-done.5
  75.6 0.5 copy-done.13
  76.1 0.2 copy-done.14
  76.3 0.5 fusion.72
  76.8 1.3 collective-permute-start.3
  78.1 7.9 collective-permute-start.2
  86.1 0.2 subtract_multiply_fusion.2
  86.3 0.6 fusion.1
  86.9 14.5 %collective-permute-done.3 = f32[1,512,128]{2,1,0:T(8,128)S(1)} collective-permute-done((f32[1,512,128]{2,1,0:T(8,128)S(1)}, f32[1,512,128]{2,1,0:T(8,128)S(1)}, u32[]{:S(2)}, u32[]{:S(2)}) %collective-permute-start.3) | collective-permute-done | bytes 262176 | tf_op jit(solution)/shard_map/ppermute | solution.py:22
  101.4 1.3 collective-permute-done.2
  102.7 0.1 fusion.6
  102.8 2.0 multiply_reduce_fusion.3
  104.8 194.2 %all-reduce.12 = (f32[]{:T(128)}, f32[]{:T(128)}) all-reduce(f32[]{:T(128)} %get-tuple-element.3, f32[]{:T(128)} %get-tuple-element.2), channel_id=1, replica_groups=mesh['test'=8,'slab'=64] {'slab'}, use_global_device_ids=true, to_apply=%region_2.3 | all-reduce | flops 2 | bytes 16 | tf_op jit(solution)/shard_map/psum | solution.py:85
  300.4 2.7 multiply_reduce_fusion.2
  303.0 188.1 %psum.51 = f32[]{:T(128)} all-reduce(f32[]{:T(128)} %get-tuple-element.8), channel_id=1, replica_groups=mesh['test'=8,'slab'=64] {'slab'}, use_global_device_ids=true, to_apply=%region_6.7 | all-reduce | flops 1 | bytes 8 | tf_op jit(solution)/shard_map/psum | solution.py:85
  492.5 1.1 multiply_add_fusion.2
  493.6 1.3 collective-permute-start.5
  494.9 7.9 collective-permute-start.4
  502.8 0.2 subtract_multiply_fusion.1
  503.0 0.6 fusion.3
  503.7 4.3 collective-permute-done.5
  508.0 0.1 fusion.7
  508.1 1.9 multiply_reduce_fusion.1
  510.0 194.4 %psum.52 = f32[]{:T(128)} all-reduce(f32[]{:T(128)} %get-tuple-element.6), channel_id=1, replica_groups=mesh['test'=8,'slab'=64] {'slab'}, use_global_device_ids=true, to_apply=%region_8.9 | all-reduce | flops 1 | bytes 8 | tf_op jit(solution)/shard_map/psum | solution.py:130
  705.6 2.0 multiply_reduce_fusion
  707.6 188.9 %psum.53 = f32[]{:T(128)} all-reduce(f32[]{:T(128)} %multiply_reduce_fusion), channel_id=1, replica_groups=mesh['test'=8,'slab'=64] {'slab'}, use_global_device_ids=true, to_apply=%region_10.11 | all-reduce | flops 1 | bytes 8 | tf_op jit(solution)/shard_map/psum | solution.py:85
  897.9 1.5 multiply_add_fusion.1
  899.4 1.3 collective-permute-start.7
  900.7 7.9 collective-permute-start.6
  908.7 0.2 subtract_multiply_fusion
  908.9 0.6 fusion.5
  909.5 0.0 copy-start.4
  909.5 4.1 collective-permute-done.7
  913.6 0.1 fusion.8
  913.8 1.1 fusion.46
  914.8 197.7 %psum.54 = f32[]{:T(128)} all-reduce(f32[]{:T(128)} %fusion.46), channel_id=1, replica_groups=mesh['test'=8,'slab'=64] {'slab'}, use_global_device_ids=true, to_apply=%region_12.13 | all-reduce | flops 1 | bytes 8 | tf_op jit(solution)/shard_map/psum | solution.py:130
  1113.9 0.1 multiply_add_fusion
  1114.0 0.0 copy-start.12
  1114.0 1.6 collective-permute-start.8
  1115.6 1.3 collective-permute-start.9
  1116.9 4.9 collective-permute-done.8
  1121.8 7.0 collective-permute-done.9
  1128.8 2.3 fusion.65
  1131.1 0.0 all-reduce.15.cloned.1.call-update
  1131.1 224.5 %all-reduce.15.cloned.1.call-done = f32[2,512,128]{2,1,0:T(8,128)} async-done(((f32[2,512,128]{2,1,0:T(8,128)}), f32[2,512,128]{2,1,0:T(8,128)}) %all-reduce.15.cloned.1.call-update) | async-done | bytes 524304 | tf_op jit(solution)/shard_map/psum | solution.py:144
  1355.6 1.9 copy.12
  (35 shorter events, 0.2 us)
Async XLA Ops:
  7.2 1.2 copy-start
  7.2 13.1 copy-start.15
  7.2 1348.4 %all-reduce.15.cloned.1.call-start = ((), (), s32[]{:S(2)}) async-start(), calls=%async_computation | async-start | bytes 1048576 | tf_op jit(solution)/shard_map/psum | solution.py:144
  8.4 12.7 copy-start.16
  9.3 26.8 %collective-permute-start = (f32[2,1,512,128]{3,2,1,0:T(8,128)}, f32[2,1,512,128]{3,2,1,0:T(8,128)S(1)}, u32[]{:S(2)}, u32[]{:S(2)}) collective-permute-start(f32[2,1,512,128]{3,2,1,0:T(8,128)} %get-tuple-element.17), channel_id=1, source_target_pairs={{0,1},{1,2},{2,3},{3,4},{4,5},{5,6},{6,7},{7,8},{8,9},{9,10},{10,1... | collective-permute-start | bytes 1572872 | tf_op jit(solution)/shard_map/ppermute | solution.py:20
  19.0 54.4 %collective-permute-start.1 = (f32[2,1,512,128]{3,2,1,0:T(8,128)S(1)}, f32[2,1,512,128]{3,2,1,0:T(8,128)S(1)}, u32[]{:S(2)}, u32[]{:S(2)}) collective-permute-start(f32[2,1,512,128]{3,2,1,0:T(8,128)S(1)} %get-tuple-element.18), channel_id=1, source_target_pairs={{1,0},{2,1},{3,2},{4,3},{5,4},{6,5},{7,6},{8,7},{9,8},{10,9},{11,1... | collective-permute-start | bytes 1572872 | tf_op jit(solution)/shard_map/ppermute | solution.py:22
  73.6 1.2 copy-start.8
  73.6 3.2 copy-start.10
  73.6 1.4 copy-start.2
  73.6 2.0 copy-start.5
  73.6 2.5 copy-start.13
  73.6 2.6 copy-start.14
  76.8 628.8 %copy-start.1 = (f32[2,512,128]{2,1,0:T(8,128)}, f32[2,512,128]{2,1,0:T(8,128)S(1)}, u32[]{:S(2)}) copy-start(f32[2,512,128]{2,1,0:T(8,128)S(1)} %get-tuple-element.13) | copy-start | bytes 1572868
  76.8 24.6 %collective-permute-start.3 = (f32[1,512,128]{2,1,0:T(8,128)S(1)}, f32[1,512,128]{2,1,0:T(8,128)S(1)}, u32[]{:S(2)}, u32[]{:S(2)}) collective-permute-start(f32[1,512,128]{2,1,0:T(8,128)S(1)} %get-tuple-element.25), channel_id=1, source_target_pairs={{1,0},{2,1},{3,2},{4,3},{5,4},{6,5},{7,6},{8,7},{9,8},{10,9},{11,1... | collective-permute-start | bytes 786440 | tf_op jit(solution)/shard_map/ppermute | solution.py:22
  78.1 24.5 %collective-permute-start.2 = (f32[1,512,128]{2,1,0:T(8,128)S(1)}, f32[1,512,128]{2,1,0:T(8,128)S(1)}, u32[]{:S(2)}, u32[]{:S(2)}) collective-permute-start(f32[1,512,128]{2,1,0:T(8,128)S(1)} %get-tuple-element.26), channel_id=1, source_target_pairs={{0,1},{1,2},{2,3},{3,4},{4,5},{5,6},{6,7},{7,8},{8,9},{9,10},{10,1... | collective-permute-start | bytes 786440 | tf_op jit(solution)/shard_map/ppermute | solution.py:20
  493.6 14.3 %collective-permute-start.5 = (f32[1,512,128]{2,1,0:T(8,128)S(1)}, f32[1,512,128]{2,1,0:T(8,128)S(1)}, u32[]{:S(2)}, u32[]{:S(2)}) collective-permute-start(f32[1,512,128]{2,1,0:T(8,128)S(1)} %get-tuple-element.23), channel_id=1, source_target_pairs={{1,0},{2,1},{3,2},{4,3},{5,4},{6,5},{7,6},{8,7},{9,8},{10,9},{11,1... | collective-permute-start | bytes 786440 | tf_op jit(solution)/shard_map/ppermute | solution.py:22
  494.9 13.1 collective-permute-start.4
  503.6 4.5 copy-start.3
  503.6 4.5 copy-start.6
  899.4 14.1 %collective-permute-start.7 = (f32[1,512,128]{2,1,0:T(8,128)S(1)}, f32[1,512,128]{2,1,0:T(8,128)S(1)}, u32[]{:S(2)}, u32[]{:S(2)}) collective-permute-start(f32[1,512,128]{2,1,0:T(8,128)S(1)} %get-tuple-element.21), channel_id=1, source_target_pairs={{1,0},{2,1},{3,2},{4,3},{5,4},{6,5},{7,6},{8,7},{9,8},{10,9},{11,1... | collective-permute-start | bytes 786440 | tf_op jit(solution)/shard_map/ppermute | solution.py:22
  900.7 12.8 collective-permute-start.6
  909.5 4.3 copy-start.4
  909.5 4.3 copy-start.7
  1113.9 14.9 %copy-start.9 = (f32[2,3,512,128]{3,2,1,0:T(8,128)S(1)}, f32[2,3,512,128]{3,2,1,0:T(8,128)}, u32[]{:S(2)}) copy-start(f32[2,3,512,128]{3,2,1,0:T(8,128)} %copy-done.8) | copy-start | bytes 4718596
  1113.9 14.9 %copy-start.11 = (f32[2,3,512,128]{3,2,1,0:T(8,128)S(1)}, f32[2,3,512,128]{3,2,1,0:T(8,128)}, u32[]{:S(2)}) copy-start(f32[2,3,512,128]{3,2,1,0:T(8,128)} %copy-done.10) | copy-start | bytes 4718596
  1114.0 17.1 %copy-start.12 = (f32[2,512,128]{2,1,0:T(8,128)}, f32[2,512,128]{2,1,0:T(8,128)S(1)}, u32[]{:S(2)}) copy-start(f32[2,512,128]{2,1,0:T(8,128)S(1)} %multiply_add_fusion) | copy-start | bytes 1572868
  1114.0 7.7 collective-permute-start.8
  1115.6 13.2 collective-permute-start.9
Sparse Core Ops, SparseCore 0:
  1131.3 224.2 all-reduce.14
where the time goes:
time: 1370 us; the launch traced here: 1360 us
  blocking collectives  963 us (70%)
  waiting for transfers between devices  310 us (23%)
  starting transfers between devices  41.5 us (3%)
  between operations  21.8 us (2%)
  other arithmetic  21.5 us (2%)
    psum x3, blocking collectives, precond_inner(): return lax.psum(jnp.sum(resid * precond), 'slab')  571 us
    psum x2, blocking collectives, on_device(): alpha = rz_now / lax.psum(jnp.sum(direction * image), 'slab')  392 us
    psum x1, waiting for transfers between devices, on_device(): gradient = lax.psum(-terms, 'test')  224 us
    ppermute x5, waiting for transfers between devices, padded_2(): lax.ppermute(head, axis, [((i + 1) % count, i) for i in range(ends)])  67.2 us
    ppermute x5, starting transfers between devices, padded_2(): lax.ppermute(tail, axis, [(i, (i + 1) % count) for i in range(ends)])  35 us
  transfers between devices with their start and end apart: 11, of which 9 were waited for; matrix products, arithmetic and copies ran while one was open for 0% of the time, Pallas kernels for 0%

commit v1 on v0

v1 whole, which is shorter than its diff:
```python
import functools

import jax
import jax.numpy as jnp
from jax import lax
from jax.experimental import pallas as pl
from jax.experimental.pallas import tpu as pltpu
from jax.sharding import PartitionSpec as P

MESH = pl.DeviceIdType.MESH
WELL_TERM = 4.0
SLABS = 64
ROWS = 512
LANES = 128
NOBS = 64
PAD = 8
BLOCK = 16
CHUNK = 128
CHUNKS = ROWS // CHUNK
HALF = ROWS // 2
PIECE = 64


class Copies:
    def __init__(self, send, recv):
        self.send, self.recv, self.count = send, recv, 0

    def start(self, src, dst, **where):
        copy = pltpu.make_async_remote_copy(
            src_ref=src,
            dst_ref=dst,
            send_sem=self.send.at[self.count],
            recv_sem=self.recv.at[self.count],
            device_id=where,
            device_id_type=MESH,
        )
        self.count += 1
        copy.start()
        return copy


N_COPIES = 2 + 4 + 2 + 2 * CHUNKS + 2 * CHUNKS + CHUNKS + 3 * 18 + 1 + 3 + 1 + 4


def rows_at(start, size=BLOCK):
    return pl.ds(start, size)


def kernel(
    lk, sto, act_in, hd, adj, pump, obs_col, obs_row, obs_val, adj_out, grad_out,
    kpad, hpad, zpad, lpad, klog, krim, faces, slopes, rim_coef, self_t, diag, inv, rhs,
    p_now, g0, g1, y1, z0r, g0r, z1r, g1r, hrim, msg, inbox, gpart, pair_in, gsum, piece_in, gfull,
    far_in, send, recv,
):
    me = lax.axis_index("slab")
    test = lax.axis_index("test")
    above, below = lax.rem(me + 1, SLABS), lax.rem(me + SLABS - 1, SLABS)
    chip, core = test // 2, lax.rem(test, 2)
    sibling = test + 1 - 2 * core
    mates = [lax.rem(test + 2 * i, 8) for i in (1, 2, 3)]
    plane_at, deep = me // 4, lax.rem(me, 4)
    col, line = lax.rem(plane_at, 4), plane_at // 4
    z_part = [plane_at * 4 + lax.rem(deep + i, 4) for i in (1, 2, 3)]
    xy_part = [
        (lax.rem(line + j, 4) * 4 + lax.rem(col + i, 4)) * 4 + deep
        for j in range(4) for i in range(4) if i or j
    ]
    barrier = pltpu.get_barrier_semaphore()
    for other in [above, below] + z_part + xy_part:
        pl.semaphore_signal(barrier, inc=1, device_id={"slab": other}, device_id_type=MESH)
    for other in [sibling] + mates:
        pl.semaphore_signal(barrier, inc=1, device_id={"test": other}, device_id_type=MESH)
    copies = Copies(send, recv)
    pending = []

    def begin(src, dst, **where):
        copy = copies.start(src, dst, **where)
        pending.append(copy)
        return copy

    own = pl.ds(pl.multiple_of(core * HALF + chip * PIECE, PIECE), PIECE)
    own_half = pl.ds(pl.multiple_of(core * HALF, HALF), HALF)

    pl.semaphore_wait(barrier, 24)
    to_above = begin(lk.at[1, own], klog.at[0, own], slab=above)
    to_below = begin(lk.at[0, own], klog.at[1, own], slab=below)
    head_copies = [
        begin(hd.at[1, pl.ds(0, HALF)], hrim.at[pl.ds(0, HALF)], slab=above),
        begin(hd.at[0, pl.ds(HALF, HALF)], hrim.at[pl.ds(HALF, HALF)], slab=below),
    ]

    low_pad = jnp.zeros((2, PAD, LANES), jnp.float32)
    for ref, fill in ((kpad, 1.0), (hpad, 0.0), (zpad, 0.0), (lpad, 0.0)):
        ref[:, pl.ds(0, PAD), :] = low_pad + fill
        ref[:, pl.ds(PAD + ROWS, PAD), :] = low_pad + fill

    offset = me * (2 * ROWS)
    cell_row = obs_col[...] // LANES - offset
    cell_lane = lax.rem(obs_col[...], LANES)
    hit = lax.broadcasted_iota(jnp.int32, (NOBS, LANES), 1) == cell_lane
    picked = jnp.zeros((NOBS, LANES), jnp.float32)
    for x in range(2):
        where_row = lax.broadcasted_iota(jnp.int32, (NOBS, ROWS), 1) + x * ROWS == cell_row
        picked = picked + jnp.dot(
            where_row.astype(jnp.float32), hd[x],
            precision=lax.Precision.HIGHEST, preferred_element_type=jnp.float32,
        )
    values = jnp.where(hit, picked - obs_val[...], 0.0)
    row_of = obs_row[...] // LANES - offset
    for x in range(2):
        where_row = lax.broadcasted_iota(jnp.int32, (ROWS, NOBS), 0) + x * ROWS == row_of
        rhs[x] = jnp.dot(
            where_row.astype(jnp.float32), values,
            precision=lax.Precision.HIGHEST, preferred_element_type=jnp.float32,
        )

    well_at = pump[0] - offset * LANES
    shape = (2, BLOCK, LANES)
    lane_no = lax.broadcasted_iota(jnp.int32, shape, 2)
    row_no = lax.broadcasted_iota(jnp.int32, shape, 1)
    cell_no = lax.broadcasted_iota(jnp.int32, shape, 0) * (ROWS * LANES) + row_no * LANES + lane_no

    def prepare(i, carry):
        at = pl.multiple_of(i * BLOCK, BLOCK)
        here = rows_at(at)
        kpad[:, rows_at(pl.multiple_of(PAD + at, 8)), :] = jnp.exp(lk[:, here, :])
        hpad[:, rows_at(pl.multiple_of(PAD + at, 8)), :] = hd[:, here, :]
        return carry

    lax.fori_loop(0, ROWS // BLOCK, prepare, 0)

    def local_terms(i, carry):
        at = pl.multiple_of(i * BLOCK, BLOCK)
        here = rows_at(at)
        k = kpad[:, rows_at(pl.multiple_of(PAD + at, 8)), :]
        total = jnp.zeros(shape, jnp.float32)
        sides = (
            (kpad[:, rows_at(PAD - 1 + at), :], row_no + at > 0),
            (kpad[:, rows_at(PAD + 1 + at), :], row_no + at < ROWS - 1),
            (pltpu.roll(k, 1, 2), lane_no > 0),
            (pltpu.roll(k, LANES - 1, 2), lane_no < LANES - 1),
        )
        for n, (other, inside) in enumerate(sides):
            both = k + other
            face = jnp.where(inside, 2.0 * k * other / both, 0.0)
            faces[n, :, here, :] = face
            slopes[n, :, here, :] = face * other / both
            total = total + face
        both = k[0] + k[1]
        face = 2.0 * k[0] * k[1] / both
        rim_coef[0, here, :] = face
        rim_coef[1, here, :] = face * k[1] / both
        rim_coef[2, here, :] = face * k[0] / both
        well = jnp.where(cell_no + at * LANES == well_at, WELL_TERM, 0.0)
        self_here = sto[:, here, :] + well
        self_t[:, here, :] = self_here
        diag[:, here, :] = self_here + total + face[None]
        active = act_in[:, here, :].astype(jnp.float32)
        rhs[:, here, :] = active * (sto[:, here, :] * adj[:, here, :] + rhs[:, here, :])
        return carry

    lax.fori_loop(0, ROWS // BLOCK, local_terms, 0)

    def gather(ref, arrived):
        for copy in arrived:
            copy.wait_recv()
        around = [begin(ref.at[:, own], ref.at[:, own], test=mate) for mate in mates]
        for copy in around:
            copy.wait_recv()
        begin(ref.at[:, own_half], ref.at[:, own_half], test=sibling).wait_recv()

    gather(klog, [to_above, to_below])

    low_edge = jnp.where(me > 0, 1.0, 0.0)
    high_edge = jnp.where(me < SLABS - 1, 1.0, 0.0)

    def rim_terms(i, carry):
        at = pl.multiple_of(i * BLOCK, BLOCK)
        here = rows_at(at)
        k = kpad[:, rows_at(pl.multiple_of(PAD + at, 8)), :]
        other = jnp.exp(klog[:, here, :])
        krim[:, here, :] = other
        both = k + other
        face = 2.0 * k * other / both
        low = face[0] * low_edge
        high = face[1] * high_edge
        rim_coef[3, here, :] = low
        rim_coef[4, here, :] = high
        rim_coef[5, here, :] = low * other[0] / both[0]
        rim_coef[6, here, :] = high * other[1] / both[1]
        rim_coef[7, here, :] = low * k[0] / both[0]
        rim_coef[8, here, :] = high * k[1] / both[1]
        active = act_in[:, here, :].astype(jnp.float32)
        fixed = 1.0 - active
        d0 = active[0] * (diag[0, here, :] + low) + fixed[0]
        d1 = active[1] * (diag[1, here, :] + high) + fixed[1]
        diag[0, here, :] = d0
        diag[1, here, :] = d1
        inv[0, here, :] = 1.0 / d0
        inv[1, here, :] = 1.0 / d1
        there = rows_at(pl.multiple_of(PAD + at, 8))
        z0 = rhs[0, here, :] / d0
        z1 = rhs[1, here, :] / d1
        zpad[0, there, :] = z0
        zpad[1, there, :] = z1
        p_now[0, here, :] = z0
        p_now[1, here, :] = z1
        return carry

    def send_rims(ref, pad, rims, chunk):
        src = pl.ds(pad + chunk * CHUNK, CHUNK)
        dst = pl.ds(chunk * CHUNK, CHUNK)
        return [
            begin(ref.at[1, src], rims.at[0, dst], slab=above),
            begin(ref.at[0, src], rims.at[1, dst], slab=below),
        ]

    per_chunk = CHUNK // BLOCK
    z_copies = []
    for chunk in range(CHUNKS):
        lax.fori_loop(chunk * per_chunk, (chunk + 1) * per_chunk, rim_terms, 0)
        z_copies.append(send_rims(zpad, PAD, z0r, chunk))

    def image_of(at, rim_low, rim_high):
        here = rows_at(at)
        there = rows_at(pl.multiple_of(PAD + at, 8))
        z = zpad[:, there, :]
        flux = faces[0, :, here, :] * (z - zpad[:, rows_at(PAD - 1 + at), :])
        flux = flux + faces[1, :, here, :] * (z - zpad[:, rows_at(PAD + 1 + at), :])
        flux = flux + faces[2, :, here, :] * (z - pltpu.roll(z, 1, 2))
        flux = flux + faces[3, :, here, :] * (z - pltpu.roll(z, LANES - 1, 2))
        across = rim_coef[0, here, :] * (z[0] - z[1])
        low = across + rim_coef[3, here, :] * (z[0] - rim_low)
        high = rim_coef[4, here, :] * (z[1] - rim_high) - across
        active = act_in[:, here, :].astype(jnp.float32)
        body = self_t[:, here, :] * z + flux
        image0 = active[0] * (body[0] + low) + (1.0 - active[0]) * z[0]
        image1 = active[1] * (body[1] + high) + (1.0 - active[1]) * z[1]
        return z, image0, image1

    zero = jnp.zeros((BLOCK, LANES), jnp.float32)

    def inner_terms(sums, z, image0, image1, d):
        rz = sums[0] + z[0] * z[0] * d[0] + z[1] * z[1] * d[1]
        pw = sums[1] + z[0] * image0 + z[1] * image1
        return rz, pw

    def all_sum(which, sums):
        first = jnp.concatenate([jnp.sum(s, axis=0, keepdims=True) for s in sums], axis=0)
        n = 0
        for stage in (z_part, xy_part):
            msg[which, n] = first
            batch = [
                begin(msg.at[which, n], inbox.at[which, n + i], slab=other)
                for i, other in enumerate(stage)
            ]
            for copy in batch:
                copy.wait_recv()
            for i in range(len(stage)):
                first = first + inbox[which, n + i]
            n += len(stage)
        total = jnp.sum(first, axis=1, keepdims=True)
        total = jnp.broadcast_to(total, (2, LANES))
        return total[0:1], total[1:2]

    def first_image(i, sums):
        at = pl.multiple_of(i * BLOCK, BLOCK)
        here = rows_at(at)
        z, image0, image1 = image_of(at, z0r[0, here, :], z0r[1, here, :])
        g0[0, here, :] = image0 * inv[0, here, :]
        g0[1, here, :] = image1 * inv[1, here, :]
        return inner_terms(sums, z, image0, image1, diag[:, here, :])

    sums = (zero, zero)
    g0_copies = []
    for chunk in range(CHUNKS):
        for copy in z_copies[chunk]:
            copy.wait_recv()
        sums = lax.fori_loop(chunk * per_chunk, (chunk + 1) * per_chunk, first_image, sums)
        g0_copies.append(send_rims(g0, 0, g0r, chunk))
    for pairs in z_copies:
        for copy in pairs:
            copy.wait_send()
    done = [id(copy) for pairs in z_copies for copy in pairs]
    pending[:] = [copy for copy in pending if id(copy) not in done]
    rz0, pw0 = all_sum(0, sums)
    alpha0 = rz0 / pw0

    def step_one(i, carry):
        at = pl.multiple_of(i * BLOCK, BLOCK)
        here = rows_at(at)
        zpad[:, rows_at(pl.multiple_of(PAD + at, 8)), :] = p_now[:, here, :] - alpha0 * g0[:, here, :]
        return carry

    lax.fori_loop(0, ROWS // BLOCK, step_one, 0)

    def second_image(i, sums):
        at = pl.multiple_of(i * BLOCK, BLOCK)
        here = rows_at(at)
        rim = z0r[:, here, :] - alpha0 * g0r[:, here, :]
        z1r[:, here, :] = rim
        z, image0, image1 = image_of(at, rim[0], rim[1])
        g1[0, here, :] = image0 * inv[0, here, :]
        g1[1, here, :] = image1 * inv[1, here, :]
        return inner_terms(sums, z, image0, image1, diag[:, here, :])

    sums = (zero, zero)
    g1_copies = []
    for chunk in range(CHUNKS):
        for copy in g0_copies[chunk]:
            copy.wait_recv()
        sums = lax.fori_loop(chunk * per_chunk, (chunk + 1) * per_chunk, second_image, sums)
        part = pl.ds(chunk * CHUNK, CHUNK)
        if chunk < CHUNKS // 2:
            g1_copies.append(begin(g1.at[1, part], g1r.at[part], slab=above))
        else:
            g1_copies.append(begin(g1.at[0, part], g1r.at[part], slab=below))
    rz1, delta1 = all_sum(1, sums)
    beta0 = rz1 / rz0
    alpha1 = rz1 / (delta1 - beta0 * rz1 / alpha0)

    def step_two(i, carry):
        at = pl.multiple_of(i * BLOCK, BLOCK)
        here = rows_at(at)
        there = rows_at(pl.multiple_of(PAD + at, 8))
        z = zpad[:, there, :]
        p0 = p_now[:, here, :]
        p1 = z + beta0 * p0
        lpad[:, there, :] = alpha0 * p0 + alpha1 * p1
        p_now[:, here, :] = p1
        zpad[:, there, :] = z - alpha1 * (g1[:, here, :] + beta0 * g0[:, here, :])
        return carry

    lax.fori_loop(0, ROWS // BLOCK, step_two, 0)

    def energy(side, i, sums):
        at = pl.multiple_of(i * BLOCK, BLOCK)
        here = rows_at(at)
        z = zpad[:, rows_at(pl.multiple_of(PAD + at, 8)), :]
        z0 = z0r[side, here, :]
        z1 = z1r[side, here, :]
        p1 = z1 + beta0 * z0
        rim = z1 - alpha1 * (g1r[here, :] + beta0 * g0r[side, here, :])
        y1[0, here, :] = rim
        y1[1, here, :] = p1
        z1r[side, here, :] = alpha0 * z0 + alpha1 * p1
        up = z - zpad[:, rows_at(PAD + 1 + at), :]
        right = z - pltpu.roll(z, LANES - 1, 2)
        across = z[0] - z[1]
        over = z[side] - rim
        square = faces[1, :, here, :] * up * up + faces[3, :, here, :] * right * right
        square = square + self_t[:, here, :] * z * z
        active = act_in[:, here, :].astype(jnp.float32)
        fixed = (1.0 - active) * z * z
        square = square + fixed
        pw = sums[1] + square[0] + square[1] + rim_coef[0, here, :] * across * across
        pw = pw + rim_coef[3 + side, here, :] * over * over
        d = diag[:, here, :]
        rz = sums[0] + z[0] * z[0] * d[0] + z[1] * z[1] * d[1]
        return rz, pw

    sums = (zero, zero)
    for chunk in range(CHUNKS):
        g1_copies[chunk].wait_recv()
        side = 0 if chunk < CHUNKS // 2 else 1
        sums = lax.fori_loop(
            chunk * per_chunk, (chunk + 1) * per_chunk, functools.partial(energy, side), sums
        )
    rz2, delta2 = all_sum(2, sums)
    beta1 = rz2 / rz1
    alpha2 = rz2 / (delta2 - beta1 * rz2 / alpha1)

    def last_step(i, carry):
        at = pl.multiple_of(i * BLOCK, BLOCK)
        here = rows_at(at)
        there = rows_at(pl.multiple_of(PAD + at, 8))
        new = lpad[:, there, :] + alpha2 * (zpad[:, there, :] + beta1 * p_now[:, here, :])
        lpad[:, there, :] = new
        adj_out[:, here, :] = new
        return carry

    lax.fori_loop(0, ROWS // BLOCK, last_step, 0)

    for copy in head_copies:
        copy.wait_recv()

    def gradient(side, i, carry):
        at = pl.multiple_of(i * BLOCK, BLOCK)
        here = rows_at(at)
        there = rows_at(pl.multiple_of(PAD + at, 8))
        lam = lpad[:, there, :]
        head = hpad[:, there, :]
        lower, upper = rows_at(PAD - 1 + at), rows_at(PAD + 1 + at)
        total = slopes[0, :, here, :] * (lam - lpad[:, lower, :]) * (head - hpad[:, lower, :])
        total = total + slopes[1, :, here, :] * (lam - lpad[:, upper, :]) * (head - hpad[:, upper, :])
        for n, turn in ((2, 1), (3, LANES - 1)):
            total = total + slopes[n, :, here, :] * (lam - pltpu.roll(lam, turn, 2)) * (
                head - pltpu.roll(head, turn, 2)
            )
        across = (lam[0] - lam[1]) * (head[0] - head[1])
        rim = z1r[side, here, :] + alpha2 * (y1[0, here, :] + beta1 * y1[1, here, :])
        over = (lam[side] - rim) * (head[side] - hrim[here, :])
        total0 = total[0] + rim_coef[1, here, :] * across
        total1 = total[1] + rim_coef[2, here, :] * across
        if side == 0:
            total0 = total0 + rim_coef[5, here, :] * over
        else:
            total1 = total1 + rim_coef[6, here, :] * over
        gpart[0, here, :] = -total0
        gpart[1, here, :] = -total1
        gpart[2, here, :] = -rim_coef[7 + side, here, :] * over
        return carry

    blocks = HALF // BLOCK
    lax.fori_loop(0, blocks, functools.partial(gradient, 0), 0)
    lax.fori_loop(blocks, 2 * blocks, functools.partial(gradient, 1), 0)

    other_half = pl.ds(pl.multiple_of((1 - core) * HALF, HALF), HALF)
    begin(gpart.at[:, other_half], pair_in, test=sibling).wait_recv()
    gsum[...] = gpart[:, own_half, :] + pair_in[...]
    spread = []
    for i, mate in enumerate(mates):
        quarter = pl.ds(pl.multiple_of(lax.rem(chip + i + 1, 4) * PIECE, PIECE), PIECE)
        spread.append(begin(gsum.at[:, quarter], piece_in.at[i], test=mate))
    for copy in spread:
        copy.wait_recv()
    quarter = pl.ds(pl.multiple_of(chip * PIECE, PIECE), PIECE)
    piece = gsum[:, quarter, :] + piece_in[0] + piece_in[1] + piece_in[2]
    far_in[0] = piece[2]
    toward = jnp.where(core == 0, below, above)
    begin(far_in.at[0], far_in.at[1], slab=toward).wait_recv()
    gets_low = jnp.where(core == 0, 0.0, 1.0)
    gfull[0, own, :] = piece[0] + gets_low * far_in[1]
    gfull[1, own, :] = piece[1] + (1.0 - gets_low) * far_in[1]
    gather(gfull, [])
    grad_out[...] = gfull[...]
    for copy in pending:
        copy.wait_send()


def on_device(
    log_conductivity, storage, active_mask, heads, adjoint_next, pump_cells, obs_cells, obs_data
):
    full = (2, ROWS, LANES)
    one = (ROWS, LANES)
    padded = (2, ROWS + 2 * PAD, LANES)
    f32 = lambda *s: pltpu.VMEM(s, jnp.float32)
    vmem = pl.BlockSpec(memory_space=pltpu.VMEM)
    adjoint, gradient = pl.pallas_call(
        kernel,
        out_shape=[jax.ShapeDtypeStruct(full, jnp.float32)] * 2,
        in_specs=[vmem] * 5 + [pl.BlockSpec(memory_space=pltpu.SMEM)] + [vmem] * 3,
        out_specs=[vmem] * 2,
        scratch_shapes=[
            f32(*padded), f32(*padded), f32(*padded), f32(*padded),
            f32(*full), f32(*full), f32(4, *full), f32(4, *full), f32(9, *one),
            f32(*full), f32(*full), f32(*full), f32(*full),
            f32(*full), f32(*full), f32(*full), f32(*full),
            f32(*full), f32(*full), f32(*full), f32(*one), f32(*one),
            f32(3, 18, 2, LANES), f32(3, 18, 2, LANES),
            f32(3, *one), f32(3, HALF, LANES), f32(3, HALF, LANES), f32(3, 3, PIECE, LANES), f32(*full),
            f32(2, PIECE, LANES),
            pltpu.SemaphoreType.DMA((N_COPIES,)),
            pltpu.SemaphoreType.DMA((N_COPIES,)),
        ],
        compiler_params=pltpu.CompilerParams(
            collective_id=0, has_side_effects=True, vmem_limit_bytes=56 << 20
        ),
    )(
        log_conductivity, storage, active_mask, heads[0], adjoint_next[0], pump_cells,
        obs_cells.reshape(NOBS, 1), obs_cells.reshape(1, NOBS), obs_data.reshape(NOBS, 1),
    )
    return adjoint[None], gradient


def solution(mesh):
    return jax.shard_map(
        on_device,
        mesh=mesh,
        in_specs=(
            P("slab", None, None),
            P("slab", None, None),
            P("slab", None, None),
            P("test", "slab", None, None),
            P("test", "slab", None, None),
            P("test"),
            P(),
            P("test", None),
        ),
        out_specs=(P("test", "slab", None, None), P("slab", None, None)),
        check_vma=False,
    )
```

time: 1370 us -> 168 us (0.12)
  blocking collectives: 963 us -> 0 us
  waiting for transfers between devices: 310 us -> 0 us
  Pallas kernels: 0 us -> 161 us
  starting transfers between devices: 41.5 us -> 0 us
  other arithmetic: 21.5 us -> 0 us
  between operations: 21.8 us -> 1.3 us
    psum x5 -> x0, blocking collectives: 963 us -> none  [the longest x3 571 us: precond_inner(): return lax.psum(jnp.sum(resid * precond), 'slab')]
    psum x1 -> x0, waiting for transfers between devices: 224 us -> none  [on_device(): gradient = lax.psum(-terms, 'test')]
    pallas_call x0 -> x1, Pallas kernels: none -> 161 us  [on_device(): pl.pallas_call(kernel, out_shape=[jax.ShapeDtypeStruct(full, jnp.float32)...]
    ppermute x10 -> x0, waiting for transfers between devices: 85.4 us -> none  [the longest x5 67.2 us: padded_2(): lax.ppermute(head, axis, [((i + 1) % count, i) for i in range(ends)])]
    ppermute x10 -> x0, starting transfers between devices: 41.4 us -> none  [the longest x5 35 us: padded_2(): lax.ppermute(tail, axis, [(i, (i + 1) % count) for i in range(ends)])]
  transfers between devices with their start and end apart: 11 -> 0, of which waited for: 9 -> 0; matrix products, arithmetic and copies ran while one was open for 0% -> 0% of each run, Pallas kernels for 0% -> 0%
where the time goes in v1:
time: 168 us
  Pallas kernels  161 us (96%)
  local copies, waits for them, and re-layouts  4.79 us (3%)
    pallas_call x1, Pallas kernels, on_device(): pl.pallas_call(kernel, out_shape=[jax.ShapeDtypeStruct(full, jnp.float32)...  161 us
    unnamed x8, local copies, waits for them, and re-layouts  3.38 us

profile of v1, /device:TPU:1, one launch (start us, length us, event | category | flops | bytes accessed | tf_op | source)
XLA Modules:
  0.0 167.5 jit_solution(2574995678029717368)
XLA Ops:
  1.3 0.0 copy-start.2
  1.3 0.6 copy-done.2
  1.9 0.0 copy-start.1
  1.9 0.7 copy.11.obs_val
  2.6 0.0 copy-done.1
  2.6 0.7 copy.10.obs_col
  3.4 161.5 %shard_map.95 = (f32[2,512,128]{2,1,0:T(8,128)}, f32[2,512,128]{2,1,0:T(8,128)}) custom-call(f32[2,512,128]{2,1,0:T(8,128)} %lk.1, f32[2,512,128]{2,1,0:T(8,128)} %sto.1, s32[2,512,128]{2,1,0:T(8,128)} %act_in.1, f32[2,512,128]{2,1,0:T(8,128)} %bitcast.6, f32[2,512,128]{2,1,0:T(8,128)} %bitcast.7, s32[1]{0:T(128)S(6)} %copy.14.pump, s32[64,1]{1,0:T(8,128)} %copy.10.obs_col, ...), custom_call_target="tpu_custom_call" | custom-call | tf_op jit(solution)/shard_map/pallas_call | solution.py:449
  164.8 0.0 copy-start
  164.8 1.9 %copy.15 = f32[1,2,512,128]{3,2,1,0:T(8,128)} copy(f32[1,2,512,128]{3,2,1,0:T(8,128)} %bitcast.8) | data formatting | bytes 1048576
  166.8 0.0 copy-done
  166.8 0.8 copy.16
Async XLA Ops:
  1.3 0.7 copy-start.2
  1.9 0.7 copy-start.1
  164.8 1.9 %copy-start = (f32[2,512,128]{2,1,0:T(8,128)S(1)}, f32[2,512,128]{2,1,0:T(8,128)}, u32[]{:S(2)}) copy-start(f32[2,512,128]{2,1,0:T(8,128)} %get-tuple-element.9) | copy-start | bytes 1572868

commit v2 on v1

--- a/solution.py
+++ b/solution.py
@@ -39,7 +39,9 @@
         return copy
 
 
-N_COPIES = 2 + 4 + 2 + 2 * CHUNKS + 2 * CHUNKS + CHUNKS + 3 * 18 + 1 + 3 + 1 + 4
+ORDER = (0, 2, 1, 3)
+EARLY = 64
+N_COPIES = 2 + 4 + 4 + 2 * CHUNKS + 2 * CHUNKS + CHUNKS + 3 * 18 + 2 + 6 + 1 + 8
 
 
 def rows_at(start, size=BLOCK):
@@ -47,8 +49,8 @@
 
 
 def kernel(
-    lk, sto, act_in, hd, adj, pump, obs_col, obs_row, obs_val, adj_out, grad_out,
-    kpad, hpad, zpad, lpad, klog, krim, faces, slopes, rim_coef, self_t, diag, inv, rhs,
+    lk_hbm, sto_hbm, act_hbm, hd_hbm, adj_hbm, pump_hbm, cells_hbm, data_hbm, adj_out, grad_out,
+    lk, sto, act_in, adj, pump, cells, data, local, kpad, hpad, zpad, lpad, klog, krim, faces, slopes, rim_coef, self_t, diag, inv, rhs,
     p_now, g0, g1, y1, z0r, g0r, z1r, g1r, hrim, msg, inbox, gpart, pair_in, gsum, piece_in, gfull,
     far_in, send, recv,
 ):
@@ -65,11 +67,21 @@
         (lax.rem(line + j, 4) * 4 + lax.rem(col + i, 4)) * 4 + deep
         for j in range(4) for i in range(4) if i or j
     ]
+    loads = [
+        pltpu.make_async_copy(src, dst, local.at[n])
+        for n, (src, dst) in enumerate((
+            (pump_hbm, pump), (cells_hbm, cells), (data_hbm, data),
+            (hd_hbm, hpad.at[:, pl.ds(PAD, ROWS)]), (lk_hbm, lk), (sto_hbm, sto), (act_hbm, act_in),
+            (adj_hbm, adj),
+        ))
+    ]
     barrier = pltpu.get_barrier_semaphore()
     for other in [above, below] + z_part + xy_part:
         pl.semaphore_signal(barrier, inc=1, device_id={"slab": other}, device_id_type=MESH)
     for other in [sibling] + mates:
         pl.semaphore_signal(barrier, inc=1, device_id={"test": other}, device_id_type=MESH)
+    for load in loads:
+        load.start()
     copies = Copies(send, recv)
     pending = []
 
@@ -82,35 +94,48 @@
     own_half = pl.ds(pl.multiple_of(core * HALF, HALF), HALF)
 
     pl.semaphore_wait(barrier, 24)
-    to_above = begin(lk.at[1, own], klog.at[0, own], slab=above)
-    to_below = begin(lk.at[0, own], klog.at[1, own], slab=below)
-    head_copies = [
-        begin(hd.at[1, pl.ds(0, HALF)], hrim.at[pl.ds(0, HALF)], slab=above),
-        begin(hd.at[0, pl.ds(HALF, HALF)], hrim.at[pl.ds(HALF, HALF)], slab=below),
-    ]
+    to_above = begin(lk_hbm.at[1, own], klog.at[0, own], slab=above)
+    to_below = begin(lk_hbm.at[0, own], klog.at[1, own], slab=below)
+
+    def send_heads(first, size):
+        up, down = pl.ds(first, size), pl.ds(HALF + first, size)
+        return [
+            begin(hd_hbm.at[1, up], hrim.at[up], slab=above),
+            begin(hd_hbm.at[0, down], hrim.at[down], slab=below),
+        ]
+
+    head_copies = send_heads(0, EARLY)
 
     low_pad = jnp.zeros((2, PAD, LANES), jnp.float32)
     for ref, fill in ((kpad, 1.0), (hpad, 0.0), (zpad, 0.0), (lpad, 0.0)):
         ref[:, pl.ds(0, PAD), :] = low_pad + fill
         ref[:, pl.ds(PAD + ROWS, PAD), :] = low_pad + fill
 
+    for load in loads:
+        load.wait()
     offset = me * (2 * ROWS)
-    cell_row = obs_col[...] // LANES - offset
-    cell_lane = lax.rem(obs_col[...], LANES)
-    hit = lax.broadcasted_iota(jnp.int32, (NOBS, LANES), 1) == cell_lane
+    eye = lax.broadcasted_iota(jnp.int32, (NOBS, NOBS), 0) == lax.broadcasted_iota(jnp.int32, (NOBS, NOBS), 1)
+
+    def upright(row):
+        return jnp.sum(jnp.where(eye, row, 0.0), axis=1, keepdims=True)
+
+    row_of = cells[...] // LANES
+    lane_of = upright((cells[...] - row_of * LANES).astype(jnp.float32))
+    row_of = row_of - offset
+    cell_row = upright(row_of.astype(jnp.float32))
+    lane_index = lax.broadcasted_iota(jnp.int32, (NOBS, LANES), 1).astype(jnp.float32)
     picked = jnp.zeros((NOBS, LANES), jnp.float32)
     for x in range(2):
-        where_row = lax.broadcasted_iota(jnp.int32, (NOBS, ROWS), 1) + x * ROWS == cell_row
+        index = lax.broadcasted_iota(jnp.int32, (NOBS, ROWS), 1) + x * ROWS
         picked = picked + jnp.dot(
-            where_row.astype(jnp.float32), hd[x],
+            (index.astype(jnp.float32) == cell_row).astype(jnp.float32), hpad[x, pl.ds(PAD, ROWS), :],
             precision=lax.Precision.HIGHEST, preferred_element_type=jnp.float32,
         )
-    values = jnp.where(hit, picked - obs_val[...], 0.0)
-    row_of = obs_row[...] // LANES - offset
+    values = jnp.where(lane_index == lane_of, picked - upright(data[...]), 0.0)
     for x in range(2):
-        where_row = lax.broadcasted_iota(jnp.int32, (ROWS, NOBS), 0) + x * ROWS == row_of
+        index = lax.broadcasted_iota(jnp.int32, (ROWS, NOBS), 0) + x * ROWS
         rhs[x] = jnp.dot(
-            where_row.astype(jnp.float32), values,
+            (index == row_of).astype(jnp.float32), values,
             precision=lax.Precision.HIGHEST, preferred_element_type=jnp.float32,
         )
 
@@ -124,7 +149,6 @@
         at = pl.multiple_of(i * BLOCK, BLOCK)
         here = rows_at(at)
         kpad[:, rows_at(pl.multiple_of(PAD + at, 8)), :] = jnp.exp(lk[:, here, :])
-        hpad[:, rows_at(pl.multiple_of(PAD + at, 8)), :] = hd[:, here, :]
         return carry
 
     lax.fori_loop(0, ROWS // BLOCK, prepare, 0)
@@ -216,10 +240,10 @@
         ]
 
     per_chunk = CHUNK // BLOCK
-    z_copies = []
-    for chunk in range(CHUNKS):
+    z_copies = {}
+    for chunk in ORDER:
         lax.fori_loop(chunk * per_chunk, (chunk + 1) * per_chunk, rim_terms, 0)
-        z_copies.append(send_rims(zpad, PAD, z0r, chunk))
+        z_copies[chunk] = send_rims(zpad, PAD, z0r, chunk)
 
     def image_of(at, rim_low, rim_high):
         here = rows_at(at)
@@ -245,7 +269,7 @@
         pw = sums[1] + z[0] * image0 + z[1] * image1
         return rz, pw
 
-    def all_sum(which, sums):
+    def all_sum(which, sums, between):
         first = jnp.concatenate([jnp.sum(s, axis=0, keepdims=True) for s in sums], axis=0)
         n = 0
         for stage in (z_part, xy_part):
@@ -254,6 +278,8 @@
                 begin(msg.at[which, n], inbox.at[which, n + i], slab=other)
                 for i, other in enumerate(stage)
             ]
+            if n == 0:
+                between()
             for copy in batch:
                 copy.wait_recv()
             for i in range(len(stage)):
@@ -272,18 +298,23 @@
         return inner_terms(sums, z, image0, image1, diag[:, here, :])
 
     sums = (zero, zero)
-    g0_copies = []
-    for chunk in range(CHUNKS):
+    g0_copies = {}
+
+    def send_g0(chunks):
+        for chunk in chunks:
+            g0_copies[chunk] = send_rims(g0, 0, g0r, chunk)
+
+    for n, chunk in enumerate(ORDER):
         for copy in z_copies[chunk]:
             copy.wait_recv()
         sums = lax.fori_loop(chunk * per_chunk, (chunk + 1) * per_chunk, first_image, sums)
-        g0_copies.append(send_rims(g0, 0, g0r, chunk))
-    for pairs in z_copies:
-        for copy in pairs:
-            copy.wait_send()
-    done = [id(copy) for pairs in z_copies for copy in pairs]
-    pending[:] = [copy for copy in pending if id(copy) not in done]
-    rz0, pw0 = all_sum(0, sums)
+        if n < 2:
+            send_g0([chunk])
+    done = [copy for chunk in ORDER for copy in z_copies[chunk]]
+    rz0, pw0 = all_sum(0, sums, lambda: send_g0(ORDER[2:]))
+    for copy in done:
+        copy.wait_send()
+    pending[:] = [copy for copy in pending if all(copy is not other for other in done)]
     alpha0 = rz0 / pw0
 
     def step_one(i, carry):
@@ -305,17 +336,23 @@
         return inner_terms(sums, z, image0, image1, diag[:, here, :])
 
     sums = (zero, zero)
-    g1_copies = []
-    for chunk in range(CHUNKS):
+    g1_copies = {}
+
+    def send_g1(chunks):
+        for chunk in chunks:
+            part = pl.ds(chunk * CHUNK, CHUNK)
+            if chunk < CHUNKS // 2:
+                g1_copies[chunk] = begin(g1.at[1, part], g1r.at[part], slab=above)
+            else:
+                g1_copies[chunk] = begin(g1.at[0, part], g1r.at[part], slab=below)
+
+    for n, chunk in enumerate(ORDER):
         for copy in g0_copies[chunk]:
             copy.wait_recv()
         sums = lax.fori_loop(chunk * per_chunk, (chunk + 1) * per_chunk, second_image, sums)
-        part = pl.ds(chunk * CHUNK, CHUNK)
-        if chunk < CHUNKS // 2:
-            g1_copies.append(begin(g1.at[1, part], g1r.at[part], slab=above))
-        else:
-            g1_copies.append(begin(g1.at[0, part], g1r.at[part], slab=below))
-    rz1, delta1 = all_sum(1, sums)
+        if n < 2:
+            send_g1([chunk])
+    rz1, delta1 = all_sum(1, sums, lambda: send_g1(ORDER[2:]))
     beta0 = rz1 / rz0
     alpha1 = rz1 / (delta1 - beta0 * rz1 / alpha0)
 
@@ -360,13 +397,13 @@
         return rz, pw
 
     sums = (zero, zero)
-    for chunk in range(CHUNKS):
+    for chunk in ORDER:
         g1_copies[chunk].wait_recv()
         side = 0 if chunk < CHUNKS // 2 else 1
         sums = lax.fori_loop(
             chunk * per_chunk, (chunk + 1) * per_chunk, functools.partial(energy, side), sums
         )
-    rz2, delta2 = all_sum(2, sums)
+    rz2, delta2 = all_sum(2, sums, lambda: head_copies.extend(send_heads(EARLY, HALF - EARLY)))
     beta1 = rz2 / rz1
     alpha2 = rz2 / (delta2 - beta1 * rz2 / alpha1)
 
@@ -376,11 +413,13 @@
         there = rows_at(pl.multiple_of(PAD + at, 8))
         new = lpad[:, there, :] + alpha2 * (zpad[:, there, :] + beta1 * p_now[:, here, :])
         lpad[:, there, :] = new
-        adj_out[:, here, :] = new
+        adj[:, here, :] = -new
         return carry
 
     lax.fori_loop(0, ROWS // BLOCK, last_step, 0)
 
+    store = pltpu.make_async_copy(adj, adj_out, local.at[0])
+    store.start()
     for copy in head_copies:
         copy.wait_recv()
 
@@ -406,9 +445,9 @@
             total0 = total0 + rim_coef[5, here, :] * over
         else:
             total1 = total1 + rim_coef[6, here, :] * over
-        gpart[0, here, :] = -total0
-        gpart[1, here, :] = -total1
-        gpart[2, here, :] = -rim_coef[7 + side, here, :] * over
+        gpart[0, here, :] = total0
+        gpart[1, here, :] = total1
+        gpart[2, here, :] = rim_coef[7 + side, here, :] * over
         return carry
 
     blocks = HALF // BLOCK
@@ -416,24 +455,48 @@
     lax.fori_loop(blocks, 2 * blocks, functools.partial(gradient, 1), 0)
 
     other_half = pl.ds(pl.multiple_of((1 - core) * HALF, HALF), HALF)
-    begin(gpart.at[:, other_half], pair_in, test=sibling).wait_recv()
-    gsum[...] = gpart[:, own_half, :] + pair_in[...]
+    quarter = pl.ds(pl.multiple_of(chip * PIECE, PIECE), PIECE)
+    parts = (pl.ds(2, 1), pl.ds(0, 2))
+    pairs = [begin(gpart.at[part, other_half], pair_in.at[part], test=sibling) for part in parts]
     spread = []
-    for i, mate in enumerate(mates):
-        quarter = pl.ds(pl.multiple_of(lax.rem(chip + i + 1, 4) * PIECE, PIECE), PIECE)
-        spread.append(begin(gsum.at[:, quarter], piece_in.at[i], test=mate))
-    for copy in spread:
+    for part, pair in zip(parts, pairs):
+        pair.wait_recv()
+        gsum[part] = gpart[part, own_half, :] + pair_in[part]
+        spread.append([
+            begin(
+                gsum.at[part, pl.ds(pl.multiple_of(lax.rem(chip + i + 1, 4) * PIECE, PIECE), PIECE)],
+                piece_in.at[i, part], test=mate,
+            )
+            for i, mate in enumerate(mates)
+        ])
+
+    def summed(part):
+        return gsum[part, quarter, :] + piece_in[0, part] + piece_in[1, part] + piece_in[2, part]
+
+    for copy in spread[0]:
         copy.wait_recv()
-    quarter = pl.ds(pl.multiple_of(chip * PIECE, PIECE), PIECE)
-    piece = gsum[:, quarter, :] + piece_in[0] + piece_in[1] + piece_in[2]
-    far_in[0] = piece[2]
+    far_in[pl.ds(0, 1)] = summed(parts[0])
     toward = jnp.where(core == 0, below, above)
-    begin(far_in.at[0], far_in.at[1], slab=toward).wait_recv()
-    gets_low = jnp.where(core == 0, 0.0, 1.0)
-    gfull[0, own, :] = piece[0] + gets_low * far_in[1]
-    gfull[1, own, :] = piece[1] + (1.0 - gets_low) * far_in[1]
-    gather(gfull, [])
-    grad_out[...] = gfull[...]
+    far = begin(far_in.at[0], far_in.at[1], slab=toward)
+    for copy in spread[1]:
+        copy.wait_recv()
+    gfull[:, own, :] = summed(parts[1])
+    around = [begin(gfull.at[core, own], gfull.at[core, own], test=mate) for mate in mates]
+    far.wait_recv()
+    gfull[1 - core, own, :] = gfull[1 - core, own, :] + far_in[1]
+    rest = [begin(gfull.at[1 - core, own], gfull.at[1 - core, own], test=mate) for mate in mates]
+    for copy in around:
+        copy.wait_recv()
+    swap = begin(gfull.at[core, own_half], gfull.at[core, own_half], test=sibling)
+    for copy in rest:
+        copy.wait_recv()
+    last = begin(gfull.at[1 - core, own_half], gfull.at[1 - core, own_half], test=sibling)
+    swap.wait_recv()
+    last.wait_recv()
+    result = pltpu.make_async_copy(gfull, grad_out, local.at[1])
+    result.start()
+    store.wait()
+    result.wait()
     for copy in pending:
         copy.wait_send()
 
@@ -445,13 +508,16 @@
     one = (ROWS, LANES)
     padded = (2, ROWS + 2 * PAD, LANES)
     f32 = lambda *s: pltpu.VMEM(s, jnp.float32)
-    vmem = pl.BlockSpec(memory_space=pltpu.VMEM)
+    anywhere = pl.BlockSpec(memory_space=pl.ANY)
     adjoint, gradient = pl.pallas_call(
         kernel,
         out_shape=[jax.ShapeDtypeStruct(full, jnp.float32)] * 2,
-        in_specs=[vmem] * 5 + [pl.BlockSpec(memory_space=pltpu.SMEM)] + [vmem] * 3,
-        out_specs=[vmem] * 2,
+        in_specs=[anywhere] * 8,
+        out_specs=[anywhere] * 2,
         scratch_shapes=[
+            f32(*full), f32(*full), pltpu.VMEM(full, jnp.int32), f32(*full),
+            pltpu.SMEM((1,), jnp.int32), pltpu.VMEM((1, NOBS), jnp.int32), f32(1, NOBS),
+            pltpu.SemaphoreType.DMA((8,)),
             f32(*padded), f32(*padded), f32(*padded), f32(*padded),
             f32(*full), f32(*full), f32(4, *full), f32(4, *full), f32(9, *one),
             f32(*full), f32(*full), f32(*full), f32(*full),
@@ -468,9 +534,9 @@
         ),
     )(
         log_conductivity, storage, active_mask, heads[0], adjoint_next[0], pump_cells,
-        obs_cells.reshape(NOBS, 1), obs_cells.reshape(1, NOBS), obs_data.reshape(NOBS, 1),
+        obs_cells.reshape(1, NOBS), obs_data,
     )
-    return adjoint[None], gradient
+    return (-adjoint)[None], -gradient
 
 
 def solution(mesh):

time: 168 us -> 146 us (0.87)
  Pallas kernels: 161 us -> 142 us
  local copies, waits for them, and re-layouts: 4.79 us -> 0.01 us
  other arithmetic: 0 us -> 2.76 us
    pallas_call x1, Pallas kernels: 161 us -> 142 us  [on_device(): pl.pallas_call(kernel, out_shape=[jax.ShapeDtypeStruct(full, jnp.float32)...]
    unnamed x8 -> x2, local copies, waits for them, and re-layouts: 3.38 us -> 0.01 us
    broadcast_in_dim x0 -> x1, other arithmetic: none -> 1.93 us  [on_device(): return ((-adjoint)[None], -gradient)]
where the time goes in v2:
time: 146 us
  Pallas kernels  142 us (97%)
  other arithmetic  2.76 us (2%)
    pallas_call x1, Pallas kernels, on_device(): pl.pallas_call(kernel, out_shape=[jax.ShapeDtypeStruct(full, jnp.float32)...  142 us

profile of v2, /device:TPU:1, one launch (start us, length us, event | category | flops | bytes accessed | tf_op | source)
XLA Modules:
  0.0 145.6 jit_solution(5157179817697419646)
XLA Ops:
  1.3 141.5 %shard_map.95 = (f32[2,512,128]{2,1,0:T(8,128)}, f32[2,512,128]{2,1,0:T(8,128)}) custom-call(f32[2,512,128]{2,1,0:T(8,128)} %lk_hbm.1, f32[2,512,128]{2,1,0:T(8,128)} %sto_hbm.1, s32[2,512,128]{2,1,0:T(8,128)} %act_hbm.1, f32[2,512,128]{2,1,0:T(8,128)} %bitcast.5, f32[2,512,128]{2,1,0:T(8,128)} %bitcast.6, s32[1]{0:T(128)S(6)} %copy.10.pump_hbm, ...), custom_call_target="tpu_custom_call" | custom-call | tf_op jit(solution)/shard_map/pallas_call | solution.py:512
  142.8 0.0 copy-start
  142.8 1.9 %negate_bitcast_fusion = f32[1,2,512,128]{3,2,1,0:T(8,128)} fusion(f32[2,512,128]{2,1,0:T(8,128)} %get-tuple-element.4), kind=kLoop, calls=%fused_computation | loop fusion | flops 131072 | bytes 1048576 | tf_op jit(solution)/shard_map/broadcast_in_dim | solution.py:539
  144.7 0.0 copy-done
  144.8 0.8 neg.7
Async XLA Ops:
  142.8 1.9 %copy-start = (f32[2,512,128]{2,1,0:T(8,128)S(1)}, f32[2,512,128]{2,1,0:T(8,128)}, u32[]{:S(2)}) copy-start(f32[2,512,128]{2,1,0:T(8,128)} %get-tuple-element.5) | copy-start | bytes 1572868

commit v3 on v2

--- a/solution.py
+++ b/solution.py
@@ -40,8 +40,11 @@
 
 
 ORDER = (0, 2, 1, 3)
-EARLY = 64
-N_COPIES = 2 + 4 + 4 + 2 * CHUNKS + 2 * CHUNKS + CHUNKS + 3 * 18 + 2 + 6 + 1 + 8
+AHEAD = 2
+STAGE = 0
+STEP_MIN = 0.5
+STEP_MAX = 3400.0
+N_COPIES = 2 + 4 + 2 + 2 * CHUNKS + 2 * CHUNKS + CHUNKS + 2 * 18 + 2 + 6 + 1 + 8
 
 
 def rows_at(start, size=BLOCK):
@@ -51,7 +54,7 @@
 def kernel(
     lk_hbm, sto_hbm, act_hbm, hd_hbm, adj_hbm, pump_hbm, cells_hbm, data_hbm, adj_out, grad_out,
     lk, sto, act_in, adj, pump, cells, data, local, kpad, hpad, zpad, lpad, klog, krim, faces, slopes, rim_coef, self_t, diag, inv, rhs,
-    p_now, g0, g1, y1, z0r, g0r, z1r, g1r, hrim, msg, inbox, gpart, pair_in, gsum, piece_in, gfull,
+    vpad, tpad, z1, v2, z0r, v1r, z1r, t1r, v2r, hrim, msg, inbox, gpart, pair_in, gsum, piece_in, gfull,
     far_in, send, recv,
 ):
     me = lax.axis_index("slab")
@@ -104,10 +107,9 @@
             begin(hd_hbm.at[0, down], hrim.at[down], slab=below),
         ]
 
-    head_copies = send_heads(0, EARLY)
 
     low_pad = jnp.zeros((2, PAD, LANES), jnp.float32)
-    for ref, fill in ((kpad, 1.0), (hpad, 0.0), (zpad, 0.0), (lpad, 0.0)):
+    for ref, fill in ((kpad, 1.0), (hpad, 0.0), (zpad, 0.0), (lpad, 0.0), (vpad, 0.0), (tpad, 0.0)):
         ref[:, pl.ds(0, PAD), :] = low_pad + fill
         ref[:, pl.ds(PAD + ROWS, PAD), :] = low_pad + fill
 
@@ -227,8 +229,6 @@
         z1 = rhs[1, here, :] / d1
         zpad[0, there, :] = z0
         zpad[1, there, :] = z1
-        p_now[0, here, :] = z0
-        p_now[1, here, :] = z1
         return carry
 
     def send_rims(ref, pad, rims, chunk):
@@ -245,12 +245,11 @@
         lax.fori_loop(chunk * per_chunk, (chunk + 1) * per_chunk, rim_terms, 0)
         z_copies[chunk] = send_rims(zpad, PAD, z0r, chunk)
 
-    def image_of(at, rim_low, rim_high):
-        here = rows_at(at)
-        there = rows_at(pl.multiple_of(PAD + at, 8))
-        z = zpad[:, there, :]
-        flux = faces[0, :, here, :] * (z - zpad[:, rows_at(PAD - 1 + at), :])
-        flux = flux + faces[1, :, here, :] * (z - zpad[:, rows_at(PAD + 1 + at), :])
+    def image_of(ref, at, rim_low, rim_high):
+        here = rows_at(at)
+        z = ref[:, rows_at(pl.multiple_of(PAD + at, 8)), :]
+        flux = faces[0, :, here, :] * (z - ref[:, rows_at(PAD - 1 + at), :])
+        flux = flux + faces[1, :, here, :] * (z - ref[:, rows_at(PAD + 1 + at), :])
         flux = flux + faces[2, :, here, :] * (z - pltpu.roll(z, 1, 2))
         flux = flux + faces[3, :, here, :] * (z - pltpu.roll(z, LANES - 1, 2))
         across = rim_coef[0, here, :] * (z[0] - z[1])
@@ -264,154 +263,160 @@
 
     zero = jnp.zeros((BLOCK, LANES), jnp.float32)
 
-    def inner_terms(sums, z, image0, image1, d):
-        rz = sums[0] + z[0] * z[0] * d[0] + z[1] * z[1] * d[1]
-        pw = sums[1] + z[0] * image0 + z[1] * image1
-        return rz, pw
-
-    def all_sum(which, sums, between):
-        first = jnp.concatenate([jnp.sum(s, axis=0, keepdims=True) for s in sums], axis=0)
-        n = 0
-        for stage in (z_part, xy_part):
-            msg[which, n] = first
-            batch = [
-                begin(msg.at[which, n], inbox.at[which, n + i], slab=other)
+    class Sum:
+        def __init__(self, which, sums):
+            rows = [jnp.sum(s, axis=0, keepdims=True) for s in sums]
+            rows = rows + [jnp.zeros((1, LANES), jnp.float32)] * (8 - len(rows))
+            self.which, self.n, self.value = which, 0, jnp.concatenate(rows, axis=0)
+
+        def start(self, stage):
+            msg[self.which, self.n] = self.value
+            self.batch = [
+                begin(msg.at[self.which, self.n], inbox.at[self.which, self.n + i], slab=other)
                 for i, other in enumerate(stage)
             ]
-            if n == 0:
-                between()
-            for copy in batch:
+
+        def finish(self):
+            for copy in self.batch:
                 copy.wait_recv()
-            for i in range(len(stage)):
-                first = first + inbox[which, n + i]
-            n += len(stage)
-        total = jnp.sum(first, axis=1, keepdims=True)
-        total = jnp.broadcast_to(total, (2, LANES))
-        return total[0:1], total[1:2]
+            for i in range(len(self.batch)):
+                self.value = self.value + inbox[self.which, self.n + i]
+            self.n += len(self.batch)
+
+        def total(self):
+            total = jnp.broadcast_to(jnp.sum(self.value, axis=1, keepdims=True), (8, LANES))
+            return [total[i:i + 1] for i in range(8)]
 
     def first_image(i, sums):
         at = pl.multiple_of(i * BLOCK, BLOCK)
         here = rows_at(at)
-        z, image0, image1 = image_of(at, z0r[0, here, :], z0r[1, here, :])
-        g0[0, here, :] = image0 * inv[0, here, :]
-        g0[1, here, :] = image1 * inv[1, here, :]
-        return inner_terms(sums, z, image0, image1, diag[:, here, :])
+        there = rows_at(pl.multiple_of(PAD + at, 8))
+        z, image0, image1 = image_of(zpad, at, z0r[0, here, :], z0r[1, here, :])
+        vpad[0, there, :] = image0 * inv[0, here, :]
+        vpad[1, there, :] = image1 * inv[1, here, :]
+        d = diag[:, here, :]
+        rz = sums[0] + z[0] * z[0] * d[0] + z[1] * z[1] * d[1]
+        return rz, sums[1] + z[0] * image0 + z[1] * image1
 
     sums = (zero, zero)
-    g0_copies = {}
-
-    def send_g0(chunks):
+    v1_copies = {}
+
+    def send_v1(chunks):
         for chunk in chunks:
-            g0_copies[chunk] = send_rims(g0, 0, g0r, chunk)
+            v1_copies[chunk] = send_rims(vpad, PAD, v1r, chunk)
 
     for n, chunk in enumerate(ORDER):
         for copy in z_copies[chunk]:
             copy.wait_recv()
         sums = lax.fori_loop(chunk * per_chunk, (chunk + 1) * per_chunk, first_image, sums)
-        if n < 2:
-            send_g0([chunk])
-    done = [copy for chunk in ORDER for copy in z_copies[chunk]]
-    rz0, pw0 = all_sum(0, sums, lambda: send_g0(ORDER[2:]))
-    for copy in done:
-        copy.wait_send()
-    pending[:] = [copy for copy in pending if all(copy is not other for other in done)]
-    alpha0 = rz0 / pw0
-
-    def step_one(i, carry):
-        at = pl.multiple_of(i * BLOCK, BLOCK)
-        here = rows_at(at)
-        zpad[:, rows_at(pl.multiple_of(PAD + at, 8)), :] = p_now[:, here, :] - alpha0 * g0[:, here, :]
+        if n < AHEAD:
+            send_v1([chunk])
+    first_sum = Sum(0, sums)
+    first_sum.start(z_part)
+    send_v1(ORDER[AHEAD:])
+
+    def second_image(i, carry):
+        at = pl.multiple_of(i * BLOCK, BLOCK)
+        here = rows_at(at)
+        _, image0, image1 = image_of(vpad, at, v1r[0, here, :], v1r[1, here, :])
+        v2[0, here, :] = image0 * inv[0, here, :]
+        v2[1, here, :] = image1 * inv[1, here, :]
         return carry
 
-    lax.fori_loop(0, ROWS // BLOCK, step_one, 0)
-
-    def second_image(i, sums):
-        at = pl.multiple_of(i * BLOCK, BLOCK)
-        here = rows_at(at)
-        rim = z0r[:, here, :] - alpha0 * g0r[:, here, :]
-        z1r[:, here, :] = rim
-        z, image0, image1 = image_of(at, rim[0], rim[1])
-        g1[0, here, :] = image0 * inv[0, here, :]
-        g1[1, here, :] = image1 * inv[1, here, :]
-        return inner_terms(sums, z, image0, image1, diag[:, here, :])
-
-    sums = (zero, zero)
-    g1_copies = {}
-
-    def send_g1(chunks):
-        for chunk in chunks:
-            part = pl.ds(chunk * CHUNK, CHUNK)
-            if chunk < CHUNKS // 2:
-                g1_copies[chunk] = begin(g1.at[1, part], g1r.at[part], slab=above)
-            else:
-                g1_copies[chunk] = begin(g1.at[0, part], g1r.at[part], slab=below)
-
+    v2_copies = {}
     for n, chunk in enumerate(ORDER):
-        for copy in g0_copies[chunk]:
+        for copy in v1_copies[chunk]:
             copy.wait_recv()
-        sums = lax.fori_loop(chunk * per_chunk, (chunk + 1) * per_chunk, second_image, sums)
-        if n < 2:
-            send_g1([chunk])
-    rz1, delta1 = all_sum(1, sums, lambda: send_g1(ORDER[2:]))
+        lax.fori_loop(chunk * per_chunk, (chunk + 1) * per_chunk, second_image, 0)
+        part = pl.ds(chunk * CHUNK, CHUNK)
+        if chunk < CHUNKS // 2:
+            v2_copies[chunk] = begin(v2.at[1, part], v2r.at[part], slab=above)
+        else:
+            v2_copies[chunk] = begin(v2.at[0, part], v2r.at[part], slab=below)
+        if n == STAGE:
+            first_sum.finish()
+            first_sum.start(xy_part)
+    first_sum.finish()
+    rz0, pw0 = first_sum.total()[:2]
+    alpha0 = jnp.clip(rz0 / pw0, STEP_MIN, STEP_MAX)
+
+    def step_one(i, sums):
+        at = pl.multiple_of(i * BLOCK, BLOCK)
+        here = rows_at(at)
+        there = rows_at(pl.multiple_of(PAD + at, 8))
+        v_one = vpad[:, there, :]
+        v_two = v2[:, here, :]
+        z_new = zpad[:, there, :] - alpha0 * v_one
+        t_new = v_one - alpha0 * v_two
+        z1[:, here, :] = z_new
+        tpad[:, there, :] = t_new
+        d = diag[:, here, :]
+        z_d, t_d, v_d = z_new * d, t_new * d, v_one * d
+        terms = (
+            z_d * z_new, z_d * t_new, t_d * t_new, t_d * v_one, v_d * v_one, t_d * v_two, v_d * v_two,
+        )
+        return tuple(s + term[0] + term[1] for s, term in zip(sums, terms))
+
+    sums = lax.fori_loop(0, ROWS // BLOCK, step_one, (zero,) * 7)
+
+    def energy(side, i, total):
+        at = pl.multiple_of(i * BLOCK, BLOCK)
+        here = rows_at(at)
+        t = tpad[:, rows_at(pl.multiple_of(PAD + at, 8)), :]
+        v_rim = v1r[side, here, :]
+        rim = v_rim - alpha0 * v2r[here, :]
+        t1r[here, :] = rim
+        z1r[here, :] = z0r[side, here, :] - alpha0 * v_rim
+        up = t - tpad[:, rows_at(PAD + 1 + at), :]
+        right = t - pltpu.roll(t, LANES - 1, 2)
+        across = t[0] - t[1]
+        over = t[side] - rim
+        square = faces[1, :, here, :] * up * up + faces[3, :, here, :] * right * right
+        square = square + self_t[:, here, :] * t * t
+        active = act_in[:, here, :].astype(jnp.float32)
+        square = square + (1.0 - active) * t * t
+        total = total + square[0] + square[1] + rim_coef[0, here, :] * across * across
+        return total + rim_coef[3 + side, here, :] * over * over
+
+    tt_energy = zero
+    for chunk in ORDER:
+        v2_copies[chunk].wait_recv()
+        side = 0 if chunk < CHUNKS // 2 else 1
+        tt_energy = lax.fori_loop(
+            chunk * per_chunk, (chunk + 1) * per_chunk, functools.partial(energy, side), tt_energy
+        )
+    last_sum = Sum(1, sums + (tt_energy,))
+    last_sum.start(z_part)
+    head_copies = send_heads(0, HALF)
+    last_sum.finish()
+    last_sum.start(xy_part)
+    last_sum.finish()
+    rz1, zt, tt, tv, vv, tw, vw, te = last_sum.total()
     beta0 = rz1 / rz0
-    alpha1 = rz1 / (delta1 - beta0 * rz1 / alpha0)
-
-    def step_two(i, carry):
+    alpha1 = jnp.clip(rz1 / (zt - beta0 * rz1 / alpha0), STEP_MIN, STEP_MAX)
+    yy = tt + beta0 * (2.0 * tv + beta0 * vv)
+    ty = tt + beta0 * tv
+    rz2 = jnp.maximum(alpha1 * alpha1 * yy - rz1, 0.0)
+    y_energy = te + beta0 * (2.0 * tw + beta0 * vw)
+    delta2 = zt - 2.0 * alpha1 * ty + alpha1 * alpha1 * y_energy
+    beta1 = rz2 / rz1
+    alpha2 = jnp.clip(rz2 / (delta2 - beta1 * rz2 / alpha1), STEP_MIN, STEP_MAX)
+
+    def rim_step(at, side):
+        here = rows_at(at)
+        z0_rim, z1_rim = z0r[side, here, :], z1r[here, :]
+        p1 = z1_rim + beta0 * z0_rim
+        z2_rim = z1_rim - alpha1 * (t1r[here, :] + beta0 * v1r[side, here, :])
+        return alpha0 * z0_rim + alpha1 * p1 + alpha2 * (z2_rim + beta1 * p1)
+
+    def last_step(i, carry):
         at = pl.multiple_of(i * BLOCK, BLOCK)
         here = rows_at(at)
         there = rows_at(pl.multiple_of(PAD + at, 8))
-        z = zpad[:, there, :]
-        p0 = p_now[:, here, :]
-        p1 = z + beta0 * p0
-        lpad[:, there, :] = alpha0 * p0 + alpha1 * p1
-        p_now[:, here, :] = p1
-        zpad[:, there, :] = z - alpha1 * (g1[:, here, :] + beta0 * g0[:, here, :])
-        return carry
-
-    lax.fori_loop(0, ROWS // BLOCK, step_two, 0)
-
-    def energy(side, i, sums):
-        at = pl.multiple_of(i * BLOCK, BLOCK)
-        here = rows_at(at)
-        z = zpad[:, rows_at(pl.multiple_of(PAD + at, 8)), :]
-        z0 = z0r[side, here, :]
-        z1 = z1r[side, here, :]
-        p1 = z1 + beta0 * z0
-        rim = z1 - alpha1 * (g1r[here, :] + beta0 * g0r[side, here, :])
-        y1[0, here, :] = rim
-        y1[1, here, :] = p1
-        z1r[side, here, :] = alpha0 * z0 + alpha1 * p1
-        up = z - zpad[:, rows_at(PAD + 1 + at), :]
-        right = z - pltpu.roll(z, LANES - 1, 2)
-        across = z[0] - z[1]
-        over = z[side] - rim
-        square = faces[1, :, here, :] * up * up + faces[3, :, here, :] * right * right
-        square = square + self_t[:, here, :] * z * z
-        active = act_in[:, here, :].astype(jnp.float32)
-        fixed = (1.0 - active) * z * z
-        square = square + fixed
-        pw = sums[1] + square[0] + square[1] + rim_coef[0, here, :] * across * across
-        pw = pw + rim_coef[3 + side, here, :] * over * over
-        d = diag[:, here, :]
-        rz = sums[0] + z[0] * z[0] * d[0] + z[1] * z[1] * d[1]
-        return rz, pw
-
-    sums = (zero, zero)
-    for chunk in ORDER:
-        g1_copies[chunk].wait_recv()
-        side = 0 if chunk < CHUNKS // 2 else 1
-        sums = lax.fori_loop(
-            chunk * per_chunk, (chunk + 1) * per_chunk, functools.partial(energy, side), sums
-        )
-    rz2, delta2 = all_sum(2, sums, lambda: head_copies.extend(send_heads(EARLY, HALF - EARLY)))
-    beta1 = rz2 / rz1
-    alpha2 = rz2 / (delta2 - beta1 * rz2 / alpha1)
-
-    def last_step(i, carry):
-        at = pl.multiple_of(i * BLOCK, BLOCK)
-        here = rows_at(at)
-        there = rows_at(pl.multiple_of(PAD + at, 8))
-        new = lpad[:, there, :] + alpha2 * (zpad[:, there, :] + beta1 * p_now[:, here, :])
+        z_0, z_1 = zpad[:, there, :], z1[:, here, :]
+        p1 = z_1 + beta0 * z_0
+        z_2 = z_1 - alpha1 * (tpad[:, there, :] + beta0 * vpad[:, there, :])
+        new = alpha0 * z_0 + alpha1 * p1 + alpha2 * (z_2 + beta1 * p1)
         lpad[:, there, :] = new
         adj[:, here, :] = -new
         return carry
@@ -437,7 +442,7 @@
                 head - pltpu.roll(head, turn, 2)
             )
         across = (lam[0] - lam[1]) * (head[0] - head[1])
-        rim = z1r[side, here, :] + alpha2 * (y1[0, here, :] + beta1 * y1[1, here, :])
+        rim = rim_step(at, side)
         over = (lam[side] - rim) * (head[side] - hrim[here, :])
         total0 = total[0] + rim_coef[1, here, :] * across
         total1 = total[1] + rim_coef[2, here, :] * across
@@ -521,9 +526,9 @@
             f32(*padded), f32(*padded), f32(*padded), f32(*padded),
             f32(*full), f32(*full), f32(4, *full), f32(4, *full), f32(9, *one),
             f32(*full), f32(*full), f32(*full), f32(*full),
-            f32(*full), f32(*full), f32(*full), f32(*full),
-            f32(*full), f32(*full), f32(*full), f32(*one), f32(*one),
-            f32(3, 18, 2, LANES), f32(3, 18, 2, LANES),
+            f32(*padded), f32(*padded), f32(*full), f32(*full),
+            f32(*full), f32(*full), f32(*one), f32(*one), f32(*one), f32(*one),
+            f32(2, 18, 8, LANES), f32(2, 18, 8, LANES),
             f32(3, *one), f32(3, HALF, LANES), f32(3, HALF, LANES), f32(3, 3, PIECE, LANES), f32(*full),
             f32(2, PIECE, LANES),
             pltpu.SemaphoreType.DMA((N_COPIES,)),

time: 146 us -> 143 us (0.979)
  Pallas kernels: 142 us -> 139 us
    pallas_call x1, Pallas kernels: 142 us -> 139 us  [on_device(): pl.pallas_call(kernel, out_shape=[jax.ShapeDtypeStruct(full, jnp.float32)...]
where the time goes in v3:
time: 143 us
  Pallas kernels  139 us (97%)
  other arithmetic  2.76 us (2%)
    pallas_call x1, Pallas kernels, on_device(): pl.pallas_call(kernel, out_shape=[jax.ShapeDtypeStruct(full, jnp.float32)...  139 us

profile of v3, /device:TPU:1, one launch (start us, length us, event | category | flops | bytes accessed | tf_op | source)
XLA Modules:
  0.0 142.9 jit_solution(11846759117106479323)
XLA Ops:
  1.3 138.9 %shard_map.95 = (f32[2,512,128]{2,1,0:T(8,128)}, f32[2,512,128]{2,1,0:T(8,128)}) custom-call(f32[2,512,128]{2,1,0:T(8,128)} %lk_hbm.1, f32[2,512,128]{2,1,0:T(8,128)} %sto_hbm.1, s32[2,512,128]{2,1,0:T(8,128)} %act_hbm.1, f32[2,512,128]{2,1,0:T(8,128)} %bitcast.5, f32[2,512,128]{2,1,0:T(8,128)} %bitcast.6, s32[1]{0:T(128)S(6)} %copy.10.pump_hbm, ...), custom_call_target="tpu_custom_call" | custom-call | tf_op jit(solution)/shard_map/pallas_call | solution.py:517
  140.2 0.0 copy-start
  140.2 1.9 %negate_bitcast_fusion = f32[1,2,512,128]{3,2,1,0:T(8,128)} fusion(f32[2,512,128]{2,1,0:T(8,128)} %get-tuple-element.4), kind=kLoop, calls=%fused_computation | loop fusion | flops 131072 | bytes 1048576 | tf_op jit(solution)/shard_map/broadcast_in_dim | solution.py:544
  142.1 0.0 copy-done
  142.1 0.8 neg.7
Async XLA Ops:
  140.2 1.9 %copy-start = (f32[2,512,128]{2,1,0:T(8,128)S(1)}, f32[2,512,128]{2,1,0:T(8,128)}, u32[]{:S(2)}) copy-start(f32[2,512,128]{2,1,0:T(8,128)} %get-tuple-element.5) | copy-start | bytes 1572868

commit v4 on v3

--- a/solution.py
+++ b/solution.py
@@ -44,7 +44,7 @@
 STAGE = 0
 STEP_MIN = 0.5
 STEP_MAX = 3400.0
-N_COPIES = 2 + 4 + 2 + 2 * CHUNKS + 2 * CHUNKS + CHUNKS + 2 * 18 + 2 + 6 + 1 + 8
+N_COPIES = 2 + 4 + 4 + 2 * CHUNKS + 2 * CHUNKS + CHUNKS + 2 * 18 + 2 + 6 + 1 + 8
 
 
 def rows_at(start, size=BLOCK):
@@ -387,9 +387,10 @@
         )
     last_sum = Sum(1, sums + (tt_energy,))
     last_sum.start(z_part)
-    head_copies = send_heads(0, HALF)
+    head_copies = send_heads(0, HALF // 2)
     last_sum.finish()
     last_sum.start(xy_part)
+    head_copies = head_copies + send_heads(HALF // 2, HALF // 2)
     last_sum.finish()
     rz1, zt, tt, tv, vv, tw, vw, te = last_sum.total()
     beta0 = rz1 / rz0

time: 143 us -> 143 us (level); the launches traced: 143 us -> 141 us
  Pallas kernels: 139 us -> 137 us
    pallas_call x1, Pallas kernels: 139 us -> 137 us  [on_device(): pl.pallas_call(kernel, out_shape=[jax.ShapeDtypeStruct(full, jnp.float32)...]
where the time goes in v4:
time: 143 us; the launch traced here: 141 us
  Pallas kernels  137 us (96%)
  other arithmetic  2.76 us (2%)
    pallas_call x1, Pallas kernels, on_device(): pl.pallas_call(kernel, out_shape=[jax.ShapeDtypeStruct(full, jnp.float32)...  137 us

profile of v4, /device:TPU:1, one launch (start us, length us, event | category | flops | bytes accessed | tf_op | source)
XLA Modules:
  0.0 141.3 jit_solution(234405663471935452)
XLA Ops:
  1.3 137.2 %shard_map.95 = (f32[2,512,128]{2,1,0:T(8,128)}, f32[2,512,128]{2,1,0:T(8,128)}) custom-call(f32[2,512,128]{2,1,0:T(8,128)} %lk_hbm.1, f32[2,512,128]{2,1,0:T(8,128)} %sto_hbm.1, s32[2,512,128]{2,1,0:T(8,128)} %act_hbm.1, f32[2,512,128]{2,1,0:T(8,128)} %bitcast.5, f32[2,512,128]{2,1,0:T(8,128)} %bitcast.6, s32[1]{0:T(128)S(6)} %copy.10.pump_hbm, ...), custom_call_target="tpu_custom_call" | custom-call | tf_op jit(solution)/shard_map/pallas_call | solution.py:518
  138.5 0.0 copy-start
  138.5 1.9 %negate_bitcast_fusion = f32[1,2,512,128]{3,2,1,0:T(8,128)} fusion(f32[2,512,128]{2,1,0:T(8,128)} %get-tuple-element.4), kind=kLoop, calls=%fused_computation | loop fusion | flops 131072 | bytes 1048576 | tf_op jit(solution)/shard_map/broadcast_in_dim | solution.py:545
  140.5 0.0 copy-done
  140.5 0.8 neg.7
Async XLA Ops:
  138.5 1.9 %copy-start = (f32[2,512,128]{2,1,0:T(8,128)S(1)}, f32[2,512,128]{2,1,0:T(8,128)}, u32[]{:S(2)}) copy-start(f32[2,512,128]{2,1,0:T(8,128)} %get-tuple-element.5) | copy-start | bytes 1572868
